TPU v7x, 256 devices: a whole 4x4x8 slice. The times are simulated.
256 devices in a mesh: rows: 64 (over y_lo, z, x), cols: 4 (over y_hi, core).
Axes of the slice: x: 4, y: 4 (y_hi: 2, y_lo: 2; y = y_hi * 2 + y_lo), z: 8, core: 2. Of those that a mesh axis runs over, the one named last changes fastest.
Arguments:
- inputs: bfloat16 [2, 256, 512, 512], P(None, 'rows', 'cols'), may hold values from -6 to 6
- tight_conv_kernel: bfloat16 [3, 3, 512, 512], P(None, None, 'rows'), may hold values from -0.09375 to 0.09375
- wide_conv_kernel: bfloat16 [3, 3, 512, 512], P(None, None, 'rows'), may hold values from -0.09375 to 0.09375
- up_weight: bfloat16 [512, 2048], P(None, 'rows'), may hold values from -0.25 to 0.25
- down_weight: bfloat16 [2048, 512], P('rows'), may hold values from -0.125 to 0.125
Outputs:
- outputs: bfloat16 [2, 256, 512, 512], P(None, 'rows', 'cols')
All inputs are finite; a program needn't handle non-finite values.
Results may differ from a plain program's by a relative error of at most 0.007.
Values may be sent and summed in bfloat16 or wider, within the bound.
No kernel may reach another device: no remote copies, remote signals or barrier semaphores. Data moves between devices by JAX's collectives and lax.ppermute only.
A program may use at most 64 MiB of HBM per device.

v0:
```python
import jax
import jax.numpy as jnp
from jax import lax
from jax.sharding import PartitionSpec as P

TIGHT_DILATION = 16
WIDE_DILATION = 64


def extended(cells, sides, width):
    for axis, dim in sides:
        count = lax.axis_size(axis)
        ends = count - 1
        head = lax.slice_in_dim(cells, 0, width, axis=dim)
        tail = lax.slice_in_dim(cells, cells.shape[dim] - width, cells.shape[dim], axis=dim)
        cells = jnp.concatenate(
            [
                lax.ppermute(tail, axis, [(i, (i + 1) % count) for i in range(ends)]),
                cells,
                lax.ppermute(head, axis, [((i + 1) % count, i) for i in range(ends)]),
            ],
            axis=dim,
        )
    return cells


def passed_along(array, axis, by):
    devices = lax.axis_size(axis)
    pairs = [(i, i + by) for i in range(devices) if 0 <= i + by < devices]
    return lax.ppermute(array, axis, pairs)


def rms_normalize(values):
    widened = values.astype(jnp.float32)
    scaled = widened * lax.rsqrt(jnp.mean(widened * widened, axis=-1, keepdims=True) + 1e-06)
    return scaled.astype(jnp.bfloat16)


def row_tap(source, offset, mover):
    row_count = source.shape[1]
    if offset >= 0:
        steps_over, remain = divmod(offset, row_count)
        nearer = mover(source, -steps_over)
        return nearer
    steps_over, remain = divmod(-offset, row_count)
    later_rows = mover(source, steps_over)
    return later_rows


def apply_convolution(normed, weight, spread, far_reach):
    col_count = normed.shape[2]
    channel_count = normed.shape[3]
    if far_reach:
        widened = extended(normed, (("cols", 2),), spread)

        def mover(source, by):
            return passed_along(source, "rows", by)

    else:
        widened = extended(normed, (("cols", 2),), spread)

        def mover(source, by):
            return passed_along(source, "rows", by)

    taps = [row_tap(widened, -spread, mover), widened, row_tap(widened, spread, mover)]
    windows = []
    for row_index in range(3):
        for col_index in range(3):
            window = taps[row_index][:, :, col_index * spread : col_index * spread + col_count]
            windows.append(window.reshape(-1, channel_count))
    zeroed = jnp.zeros((windows[0].shape[0], weight.shape[3]), jnp.float32)

    def add_taps(summed, piece):
        for tap_index in range(9):
            row_index, col_index = divmod(tap_index, 3)
            part = windows[tap_index]
            summed = summed + jnp.dot(
                part, piece[row_index, col_index], preferred_element_type=jnp.float32
            )
        return summed

    if far_reach:
        summed = add_taps(zeroed, lax.all_gather(weight, "rows", axis=2, tiled=True))
    else:
        summed = add_taps(zeroed, lax.all_gather(weight, "rows", axis=2, tiled=True))
    return summed.reshape(normed.shape)


def make_adder(features, pieces):
    up_piece, down_piece = pieces
    product = lax.dot_general(
        features, up_piece, (((1,), (1,)), ((), ())), preferred_element_type=jnp.float32
    )
    hidden = jax.nn.gelu(product).astype(jnp.bfloat16)
    return jnp.dot(hidden, down_piece, preferred_element_type=jnp.float32)


def feed_forward(normed_rows, up_weight, down_weight):
    up_rows = up_weight.T
    return make_adder(
        normed_rows,
        (
            lax.all_gather(up_rows, "rows", axis=0, tiled=True),
            lax.all_gather(down_weight, "rows", axis=0, tiled=True),
        ),
    )


def shards(inputs, tight_conv_kernel, wide_conv_kernel, up_weight, down_weight):
    tight_conv_result = (
        inputs.astype(jnp.float32)
        + apply_convolution(rms_normalize(inputs), tight_conv_kernel, TIGHT_DILATION, False)
    ).astype(jnp.bfloat16)
    wide_conv_result = (
        tight_conv_result.astype(jnp.float32)
        + apply_convolution(rms_normalize(tight_conv_result), wide_conv_kernel, WIDE_DILATION, True)
    ).astype(jnp.bfloat16)
    mlp_rows = rms_normalize(wide_conv_result).reshape(-1, wide_conv_result.shape[3])
    branch = feed_forward(mlp_rows, up_weight, down_weight)
    return (wide_conv_result.astype(jnp.float32) + branch.reshape(wide_conv_result.shape)).astype(
        jnp.bfloat16
    )


def solution(mesh):
    placed = (
        P(None, "rows", "cols", None),
        P(None, None, "rows", None),
        P(None, None, "rows", None),
        P(None, "rows"),
        P("rows", None),
    )
    return jax.shard_map(
        shards, mesh=mesh, in_specs=placed, out_specs=P(None, "rows", "cols", None), check_vma=False
    )
```

profile of v0, /device:TPU:16, one launch (start us, length us, event | category | flops | bytes accessed | tf_op | source)
XLA Modules:
  0.0 1360.5 jit_solution(9043071128753244014)
XLA Ops:
  6.5 0.7 all-gather.5.cloned.1.call-update
  7.3 0.0 all-gather.7.cloned.1.call-start
  7.3 0.7 all-gather.7.cloned.1.call-update
  8.0 0.0 all-gather.11.cloned.1.call-start
  8.1 1.5 fusion.10
  9.6 1.5 fusion.11
  11.1 1.9 collective-permute-start
  13.1 5.1 collective-permute-start.1
  18.2 0.7 collective-permute-done
  18.9 1.8 collective-permute-done.1
  20.7 1.1 pad_maximum_fusion.1
  21.9 1.3 collective-permute-start.3
  23.2 4.6 collective-permute-start.2
  27.8 0.0 all-gather.11.cloned.1.call-update
  27.8 0.0 all-gather.9.cloned.1.call-start
  27.9 2.1 pad_maximum_fusion.5
  30.0 27.6 %collective-permute-done.3 = bf16[2,4,160,512]{3,2,1,0:T(8,128)(2,1)} collective-permute-done((bf16[2,4,160,512]{3,2,1,0:T(8,128)(2,1)}, bf16[2,4,160,512]{3,2,1,0:T(8,128)(2,1)}, u32[]{:S(2)}, u32[]{:S(2)}) %collective-permute-start.3) | collective-permute-done | bytes 1310752 | tf_op jit(solution)/shard_map/ppermute | solution.py:30
  57.6 3.8 fusion.47
  61.4 1.8 fusion.48
  63.3 253.5 %all-gather.5.cloned.1.call-done = bf16[3,3,512,512]{3,2,1,0:T(8,128)(2,1)} async-done(((bf16[3,3,8,512]{3,2,1,0:T(8,128)(2,1)}), bf16[3,3,512,512]{3,2,1,0:T(8,128)(2,1)}) %all-gather.5.cloned.1.call-update) | async-done | bytes 4718608 | tf_op jit(solution)/shard_map/all_gather | solution.py:85
  316.7 2.2 fusion.31
  319.0 1.8 fusion.32
  320.8 0.7 fusion.36
  321.5 0.5 copy-done.7
  322.0 0.7 fusion.37
  322.7 0.1 copy-done.6
  322.8 0.7 fusion.38
  323.5 0.4 copy-done.3
  324.0 0.7 fusion.33
  324.7 0.7 fusion.35
  325.4 0.7 fusion.34
  326.1 0.5 copy-done.4
  326.6 1.2 add_add_fusion.1
  327.8 0.1 copy-done
  327.8 0.4 fusion.13
  328.2 0.3 fusion.14
  328.5 0.1 fusion.49
  328.6 1.9 collective-permute-start.4
  330.6 5.1 collective-permute-start.5
  335.7 6.6 collective-permute-done.4
  342.3 1.6 collective-permute-done.5
  343.9 1.5 pad_maximum_fusion
  345.4 1.3 collective-permute-start.7
  346.7 9.9 collective-permute-start.6
  356.6 344.9 %all-gather.7.cloned.1.call-done = bf16[3,3,512,512]{3,2,1,0:T(8,128)(2,1)} async-done(((bf16[3,3,8,512]{3,2,1,0:T(8,128)(2,1)}), bf16[3,3,512,512]{3,2,1,0:T(8,128)(2,1)}) %all-gather.7.cloned.1.call-update) | async-done | bytes 4718608 | tf_op jit(solution)/shard_map/all_gather | solution.py:83
  701.5 1.9 fusion.25
  703.4 0.2 pad_maximum_fusion.3
  703.7 0.4 copy-done.1
  704.0 0.7 fusion.26
  704.7 0.7 fusion.24
  705.5 2.1 fusion.45
  707.5 0.7 fusion.22
  708.2 0.7 fusion.23
  709.0 2.2 fusion.46
  711.2 0.7 fusion.27
  711.9 0.7 fusion.28
  712.6 0.7 fusion.29
  713.3 1.2 add_add_fusion
  714.5 0.4 fusion.16
  714.9 0.3 fusion.17
  715.2 328.8 %all-gather.11.cloned.1.call-done = bf16[2048,512]{1,0:T(8,128)(2,1)} async-done(((bf16[32,512]{1,0:T(8,128)(2,1)}), bf16[2048,512]{1,0:T(8,128)(2,1)}) %all-gather.11.cloned.1.call-update) | async-done | bytes 2097168 | tf_op jit(solution)/shard_map/all_gather | solution.py:104
  1044.0 298.9 %all-gather.9.cloned.1.call-done = bf16[2048,512]{1,0:T(8,128)(2,1)} async-done(((bf16[32,512]{1,0:T(8,128)(2,1)}), bf16[2048,512]{1,0:T(8,128)(2,1)}) %all-gather.9.cloned.1.call-update) | async-done | bytes 2097168 | tf_op jit(solution)/shard_map/all_gather | solution.py:103
  1342.9 8.2 fusion.8
  1351.0 2.9 fusion.18
  (23 shorter events, 0.1 us)
Async XLA Ops:
  6.5 310.2 %all-gather.5.cloned.1.call-start = ((), (), s32[]{:S(2)}) async-start(), calls=%async_computation | async-start | bytes 4792320 | tf_op jit(solution)/shard_map/all_gather | solution.py:85
  7.3 694.3 %all-gather.7.cloned.1.call-start = ((), (), s32[]{:S(2)}) async-start(), calls=%async_computation.1 | async-start | bytes 4792320 | tf_op jit(solution)/shard_map/all_gather | solution.py:83
  8.0 1036.0 %all-gather.11.cloned.1.call-start = ((), (), s32[]{:S(2)}) async-start(), calls=%async_computation.3 | async-start | bytes 2129920 | tf_op jit(solution)/shard_map/all_gather | solution.py:104
  11.1 7.8 collective-permute-start
  13.1 7.7 collective-permute-start.1
  20.7 7.1 copy-start.9
  21.9 35.7 %collective-permute-start.3 = (bf16[2,4,160,512]{3,2,1,0:T(8,128)(2,1)}, bf16[2,4,160,512]{3,2,1,0:T(8,128)(2,1)}, u32[]{:S(2)}, u32[]{:S(2)}) collective-permute-start(bf16[2,4,160,512]{3,2,1,0:T(8,128)(2,1)} %pad_maximum_fusion.1), channel_id=1, source_target_pairs={{16,0},{20,4},{24,8},{28,12},{32,16},{36,20},{40,24},{44,28},{48,3... | collective-permute-start | bytes 3932168 | tf_op jit(solution)/shard_map/ppermute | solution.py:30
  23.2 38.2 %collective-permute-start.2 = (bf16[2,4,160,512]{3,2,1,0:T(8,128)(2,1)}, bf16[2,4,160,512]{3,2,1,0:T(8,128)(2,1)S(1)}, u32[]{:S(2)}, u32[]{:S(2)}) collective-permute-start(bf16[2,4,160,512]{3,2,1,0:T(8,128)(2,1)} %pad_maximum_fusion.1), channel_id=1, source_target_pairs={{0,16},{4,20},{8,24},{12,28},{16,32},{20,36},{24,40},{28,44},{32,4... | collective-permute-start | bytes 3932168 | tf_op jit(solution)/shard_map/ppermute | solution.py:30
  27.8 1315.0 %all-gather.9.cloned.1.call-start = ((), (), s32[]{:S(2)}) async-start(), calls=%async_computation.2 | async-start | bytes 2129920 | tf_op jit(solution)/shard_map/all_gather | solution.py:103
  63.2 255.7 %copy-start.5 = (bf16[2,4,128,512]{3,2,1,0:T(8,128)(2,1)S(1)}, bf16[2,4,128,512]{3,2,1,0:T(8,128)(2,1)}, u32[]{:S(2)}) copy-start(bf16[2,4,128,512]{3,2,1,0:T(8,128)(2,1)} %get-tuple-element.17) | copy-start | bytes 3145732
  316.7 4.1 copy-start.2
  319.0 1.9 copy-start.8
  320.8 1.2 copy-start.7
  321.5 1.3 copy-start.6
  322.7 1.3 copy-start.3
  325.4 1.2 copy-start.4
  326.6 1.2 copy-start
  328.6 13.7 %collective-permute-start.4 = (bf16[2,4,64,512]{3,2,1,0:T(8,128)(2,1)S(1)}, bf16[2,4,64,512]{3,2,1,0:T(8,128)(2,1)S(1)}, u32[]{:S(2)}, u32[]{:S(2)}) collective-permute-start(bf16[2,4,64,512]{3,2,1,0:T(8,128)(2,1)S(1)} %get-tuple-element.23), channel_id=1, source_target_pairs={{0,1},{1,2},{2,3},{4,5},{5,6},{6,7},{8,9},{9,10},{10,11},{12,13},{... | collective-permute-start | bytes 1572872 | tf_op jit(solution)/shard_map/ppermute | solution.py:18
  330.6 13.3 collective-permute-start.5
  345.4 360.0 %collective-permute-start.7 = (bf16[2,4,256,512]{3,2,1,0:T(8,128)(2,1)}, bf16[2,4,256,512]{3,2,1,0:T(8,128)(2,1)}, u32[]{:S(2)}, u32[]{:S(2)}) collective-permute-start(bf16[2,4,256,512]{3,2,1,0:T(8,128)(2,1)} %pad_maximum_fusion), channel_id=1, source_target_pairs={{64,0},{68,4},{72,8},{76,12},{80,16},{84,20},{88,24},{92,28},{96,3... | collective-permute-start | bytes 6291464 | tf_op jit(solution)/shard_map/ppermute | solution.py:30
  346.7 362.2 %collective-permute-start.6 = (bf16[2,4,256,512]{3,2,1,0:T(8,128)(2,1)}, bf16[2,4,256,512]{3,2,1,0:T(8,128)(2,1)}, u32[]{:S(2)}, u32[]{:S(2)}) collective-permute-start(bf16[2,4,256,512]{3,2,1,0:T(8,128)(2,1)} %pad_maximum_fusion), channel_id=1, source_target_pairs={{0,64},{4,68},{8,72},{12,76},{16,80},{20,84},{24,88},{28,92},{32,9... | collective-permute-start | bytes 6291464 | tf_op jit(solution)/shard_map/ppermute | solution.py:30
  701.5 2.5 copy-start.1
Sparse Core Ops, SparseCore 0:
  9.1 307.5 all-gather.4
  318.5 382.9 all-gather.6
  703.3 340.5 all-gather.10
  1045.6 297.1 all-gather.8
where the time goes:
time: 1360 us
  waiting for transfers between devices  1270 us (93%)
  starting transfers between devices  31.3 us (2%)
  matrix products  25.5 us (2%)
    all_gather x2, waiting for transfers between devices, apply_convolution(): lax.all_gather(weight, 'rows', axis=2, tiled=True)  598 us
    all_gather x1, waiting for transfers between devices, feed_forward(): lax.all_gather(down_weight, 'rows', axis=0, tiled=True)  329 us
    all_gather x1, waiting for transfers between devices, feed_forward(): lax.all_gather(up_rows, 'rows', axis=0, tiled=True)  299 us
    ppermute x4, waiting for transfers between devices, passed_along(): return lax.ppermute(array, axis, pairs)  27.6 us
  transfers between devices with their start and end apart: 12, of which 9 were waited for; matrix products, arithmetic and copies ran while one was open for 3% of the time, Pallas kernels for 0%

commit v1 on v0

--- a/solution.py
+++ b/solution.py
@@ -2,9 +2,18 @@
 import jax.numpy as jnp
 from jax import lax
 from jax.sharding import PartitionSpec as P
+from jax.lax import all_to_all, axis_size
 
 TIGHT_DILATION = 16
 WIDE_DILATION = 64
+
+
+def convert_the_map(x_local):
+    inbox = []
+    for _ in range(axis_size("rows")):
+        inbox.append(x_local)
+    mat_out = jnp.concatenate(all_to_all(jnp.stack(inbox, 0), "rows", 0, 0), 2)
+    return mat_out
 
 
 def extended(cells, sides, width):
@@ -82,7 +91,7 @@
     if far_reach:
         summed = add_taps(zeroed, lax.all_gather(weight, "rows", axis=2, tiled=True))
     else:
-        summed = add_taps(zeroed, lax.all_gather(weight, "rows", axis=2, tiled=True))
+        summed = add_taps(zeroed, convert_the_map(weight))
     return summed.reshape(normed.shape)
 
 

time: 1360 us -> 1070 us (0.79)
  waiting for transfers between devices: 1270 us -> 963 us
  starting transfers between devices: 31.3 us -> 45.3 us
    all_gather x2 -> x1, waiting for transfers between devices: 598 us -> 141 us  [apply_convolution(): lax.all_gather(weight, 'rows', axis=2, tiled=True)]
    ppermute x4, waiting for transfers between devices: 27.6 us -> 132 us  [passed_along(): return lax.ppermute(array, axis, pairs)]
    all_gather x1, waiting for transfers between devices: 299 us -> 376 us  [feed_forward(): lax.all_gather(up_rows, 'rows', axis=0, tiled=True)]
    all_gather x1, waiting for transfers between devices: 329 us -> 299 us  [feed_forward(): lax.all_gather(down_weight, 'rows', axis=0, tiled=True)]
  transfers between devices with their start and end apart: 12 -> 12, of which waited for: 9 -> 7; matrix products, arithmetic and copies ran while one was open for 3% -> 4% of each run, Pallas kernels for 0% -> 0%
where the time goes in v1:
time: 1070 us
  waiting for transfers between devices  963 us (90%)
  starting transfers between devices  45.3 us (4%)
  matrix products  22.3 us (2%)
  local copies, waits for them, and re-layouts  20.4 us (2%)
  between operations  13.4 us (1%)
    all_gather x1, waiting for transfers between devices, feed_forward(): lax.all_gather(up_rows, 'rows', axis=0, tiled=True)  376 us
    all_gather x1, waiting for transfers between devices, feed_forward(): lax.all_gather(down_weight, 'rows', axis=0, tiled=True)  299 us
    all_gather x1, waiting for transfers between devices, apply_convolution(): lax.all_gather(weight, 'rows', axis=2, tiled=True)  141 us
    ppermute x4, waiting for transfers between devices, passed_along(): return lax.ppermute(array, axis, pairs)  132 us
  transfers between devices with their start and end apart: 12, of which 7 were waited for; matrix products, arithmetic and copies ran while one was open for 4% of the time, Pallas kernels for 0%

profile of v1, /device:TPU:16, one launch (start us, length us, event | category | flops | bytes accessed | tf_op | source)
XLA Modules:
  0.0 1073.0 jit_solution(9039446056064633297)
XLA Ops:
  6.5 0.7 all-gather.4.cloned.1.call-update
  7.3 3.3 stack.2
  10.5 13.0 %all-to-all-start = ((bf16[64,3,3,8,512]{4,3,2,1,0:T(8,128)(2,1)}), bf16[64,3,3,8,512]{4,3,2,1,0:T(8,128)(2,1)}, u32[]{:S(2)}, u32[]{:S(2)}) async-start(bf16[64,3,3,8,512]{4,3,2,1,0:T(8,128)(2,1)} %stack.2), calls=%async_computation | async-start | bytes 9437184 | tf_op jit(solution)/shard_map/all_to_all | solution.py:15
  23.6 0.0 all-gather.6.cloned.1.call-start
  23.6 0.3 fusion.10
  23.9 0.3 fusion.11
  24.2 1.9 collective-permute-start
  26.2 5.1 collective-permute-start.1
  31.3 7.1 collective-permute-done
  38.4 1.2 pad_maximum_fusion.1
  39.6 1.3 collective-permute-start.3
  40.9 5.6 collective-permute-start.2
  46.5 0.0 all-gather.6.cloned.1.call-update
  46.5 0.0 all-gather.8.cloned.1.call-start
  46.6 1.2 pad_maximum_fusion.5
  47.8 131.6 %collective-permute-done.3 = bf16[2,4,160,512]{3,2,1,0:T(8,128)(2,1)} collective-permute-done((bf16[2,4,160,512]{3,2,1,0:T(8,128)(2,1)}, bf16[2,4,160,512]{3,2,1,0:T(8,128)(2,1)}, u32[]{:S(2)}, u32[]{:S(2)}) %collective-permute-start.3) | collective-permute-done | bytes 1310752 | tf_op jit(solution)/shard_map/ppermute | solution.py:39
  179.4 3.7 fusion.47
  183.1 3.6 fusion.48
  186.8 2.8 copy.8
  189.7 0.7 fusion.31
  190.4 0.5 copy-done.4
  190.9 0.7 fusion.32
  191.6 0.1 copy-done.8
  191.7 0.7 fusion.36
  192.4 0.4 copy-done.7
  192.8 0.7 fusion.37
  193.5 0.2 copy-done.6
  193.7 0.7 fusion.38
  194.4 0.4 copy-done.2
  194.8 0.7 fusion.33
  195.5 0.7 fusion.35
  196.2 0.7 fusion.34
  196.9 0.5 copy-done.3
  197.4 1.5 add_add_fusion.1
  198.9 0.4 fusion.13
  199.4 0.3 fusion.14
  199.7 0.1 fusion.49
  199.8 1.9 collective-permute-start.4
  201.7 5.1 collective-permute-start.5
  206.9 6.2 collective-permute-done.4
  213.1 1.9 collective-permute-done.5
  214.9 1.5 pad_maximum_fusion
  216.5 1.3 collective-permute-start.7
  217.8 9.9 collective-permute-start.6
  227.7 141.0 %all-gather.4.cloned.1.call-done = bf16[3,3,512,512]{3,2,1,0:T(8,128)(2,1)} async-done(((bf16[3,3,8,512]{3,2,1,0:T(8,128)(2,1)}), bf16[3,3,512,512]{3,2,1,0:T(8,128)(2,1)}) %all-gather.4.cloned.1.call-update) | async-done | bytes 4718608 | tf_op jit(solution)/shard_map/all_gather | solution.py:92
  368.7 1.9 fusion.25
  370.6 0.2 pad_maximum_fusion.3
  370.8 0.4 copy-done.1
  371.2 0.7 fusion.26
  371.9 0.7 fusion.24
  372.6 2.1 fusion.45
  374.7 0.7 fusion.22
  375.4 0.7 fusion.23
  376.1 2.2 fusion.46
  378.4 0.7 fusion.27
  379.1 0.7 fusion.28
  379.8 0.7 fusion.29
  380.5 1.2 add_add_fusion
  381.6 0.4 fusion.16
  382.1 1.3 fusion.17
  383.3 375.6 %all-gather.6.cloned.1.call-done = bf16[2048,512]{1,0:T(8,128)(2,1)} async-done(((bf16[32,512]{1,0:T(8,128)(2,1)}), bf16[2048,512]{1,0:T(8,128)(2,1)}) %all-gather.6.cloned.1.call-update) | async-done | bytes 2097168 | tf_op jit(solution)/shard_map/all_gather | solution.py:112
  758.9 299.0 %all-gather.8.cloned.1.call-done = bf16[2048,512]{1,0:T(8,128)(2,1)} async-done(((bf16[32,512]{1,0:T(8,128)(2,1)}), bf16[2048,512]{1,0:T(8,128)(2,1)}) %all-gather.8.cloned.1.call-update) | async-done | bytes 2097168 | tf_op jit(solution)/shard_map/all_gather | solution.py:113
  1058.0 7.2 fusion.8
  1065.1 1.3 fusion.18
  (22 shorter events, 0.1 us)
Async XLA Ops:
  6.5 362.2 %all-gather.4.cloned.1.call-start = ((), (), s32[]{:S(2)}) async-start(), calls=%async_computation.1 | async-start | bytes 4792320 | tf_op jit(solution)/shard_map/all_gather | solution.py:92
  10.5 13.1 %copy-start = (bf16[2,4,128,512]{3,2,1,0:T(8,128)(2,1)S(1)}, bf16[2,4,128,512]{3,2,1,0:T(8,128)(2,1)}, u32[]{:S(2)}) copy-start(bf16[2,4,128,512]{3,2,1,0:T(8,128)(2,1)} %param.5) | copy-start | bytes 3145732
  10.5 176.3 %all-to-all-start = ((bf16[64,3,3,8,512]{4,3,2,1,0:T(8,128)(2,1)}), bf16[64,3,3,8,512]{4,3,2,1,0:T(8,128)(2,1)}, u32[]{:S(2)}, u32[]{:S(2)}) async-start(bf16[64,3,3,8,512]{4,3,2,1,0:T(8,128)(2,1)} %stack.2), calls=%async_computation | async-start | bytes 9437184 | tf_op jit(solution)/shard_map/all_to_all | solution.py:15
  23.6 735.4 %all-gather.6.cloned.1.call-start = ((), (), s32[]{:S(2)}) async-start(), calls=%async_computation.2 | async-start | bytes 2129920 | tf_op jit(solution)/shard_map/all_gather | solution.py:112
  24.2 14.1 %collective-permute-start = (bf16[2,4,16,512]{3,2,1,0:T(8,128)(2,1)S(1)}, bf16[2,4,16,512]{3,2,1,0:T(8,128)(2,1)S(1)}, u32[]{:S(2)}, u32[]{:S(2)}) collective-permute-start(bf16[2,4,16,512]{3,2,1,0:T(8,128)(2,1)S(1)} %get-tuple-element.27), channel_id=1, source_target_pairs={{0,1},{1,2},{2,3},{4,5},{5,6},{6,7},{8,9},{9,10},{10,11},{12,13},{... | collective-permute-start | bytes 393224 | tf_op jit(solution)/shard_map/ppermute | solution.py:27
  26.2 12.2 %collective-permute-start.1 = (bf16[2,4,16,512]{3,2,1,0:T(8,128)(2,1)S(1)}, bf16[2,4,16,512]{3,2,1,0:T(8,128)(2,1)S(1)}, u32[]{:S(2)}, u32[]{:S(2)}) collective-permute-start(bf16[2,4,16,512]{3,2,1,0:T(8,128)(2,1)S(1)} %get-tuple-element.28), channel_id=1, source_target_pairs={{1,0},{2,1},{3,2},{5,4},{6,5},{7,6},{9,8},{10,9},{11,10},{13,12},{... | collective-permute-start | bytes 393224 | tf_op jit(solution)/shard_map/ppermute | solution.py:29
  39.6 139.8 %collective-permute-start.3 = (bf16[2,4,160,512]{3,2,1,0:T(8,128)(2,1)}, bf16[2,4,160,512]{3,2,1,0:T(8,128)(2,1)}, u32[]{:S(2)}, u32[]{:S(2)}) collective-permute-start(bf16[2,4,160,512]{3,2,1,0:T(8,128)(2,1)} %pad_maximum_fusion.1), channel_id=1, source_target_pairs={{16,0},{20,4},{24,8},{28,12},{32,16},{36,20},{40,24},{44,28},{48,3... | collective-permute-start | bytes 3932168 | tf_op jit(solution)/shard_map/ppermute | solution.py:39
  40.9 142.3 %collective-permute-start.2 = (bf16[2,4,160,512]{3,2,1,0:T(8,128)(2,1)}, bf16[2,4,160,512]{3,2,1,0:T(8,128)(2,1)}, u32[]{:S(2)}, u32[]{:S(2)}) collective-permute-start(bf16[2,4,160,512]{3,2,1,0:T(8,128)(2,1)} %pad_maximum_fusion.1), channel_id=1, source_target_pairs={{0,16},{4,20},{8,24},{12,28},{16,32},{20,36},{24,40},{28,44},{32,4... | collective-permute-start | bytes 3932168 | tf_op jit(solution)/shard_map/ppermute | solution.py:39
  46.5 1011.4 %all-gather.8.cloned.1.call-start = ((), (), s32[]{:S(2)}) async-start(), calls=%async_computation.3 | async-start | bytes 2129920 | tf_op jit(solution)/shard_map/all_gather | solution.py:113
  186.8 2.9 copy-start.5
  189.6 1.2 copy-start.4
  190.4 1.3 copy-start.8
  191.6 1.3 copy-start.7
  192.4 1.3 copy-start.6
  193.5 1.3 copy-start.2
  196.2 1.2 copy-start.3
  199.8 13.3 %collective-permute-start.4 = (bf16[2,4,64,512]{3,2,1,0:T(8,128)(2,1)S(1)}, bf16[2,4,64,512]{3,2,1,0:T(8,128)(2,1)S(1)}, u32[]{:S(2)}, u32[]{:S(2)}) collective-permute-start(bf16[2,4,64,512]{3,2,1,0:T(8,128)(2,1)S(1)} %get-tuple-element.23), channel_id=1, source_target_pairs={{0,1},{1,2},{2,3},{4,5},{5,6},{6,7},{8,9},{9,10},{10,11},{12,13},{... | collective-permute-start | bytes 1572872 | tf_op jit(solution)/shard_map/ppermute | solution.py:27
  201.7 13.2 %collective-permute-start.5 = (bf16[2,4,64,512]{3,2,1,0:T(8,128)(2,1)S(1)}, bf16[2,4,64,512]{3,2,1,0:T(8,128)(2,1)S(1)}, u32[]{:S(2)}, u32[]{:S(2)}) collective-permute-start(bf16[2,4,64,512]{3,2,1,0:T(8,128)(2,1)S(1)} %get-tuple-element.24), channel_id=1, source_target_pairs={{1,0},{2,1},{3,2},{5,4},{6,5},{7,6},{9,8},{10,9},{11,10},{13,12},{... | collective-permute-start | bytes 1572872 | tf_op jit(solution)/shard_map/ppermute | solution.py:29
  216.5 156.1 %collective-permute-start.7 = (bf16[2,4,256,512]{3,2,1,0:T(8,128)(2,1)}, bf16[2,4,256,512]{3,2,1,0:T(8,128)(2,1)}, u32[]{:S(2)}, u32[]{:S(2)}) collective-permute-start(bf16[2,4,256,512]{3,2,1,0:T(8,128)(2,1)} %pad_maximum_fusion), channel_id=1, source_target_pairs={{64,0},{68,4},{72,8},{76,12},{80,16},{84,20},{88,24},{92,28},{96,3... | collective-permute-start | bytes 6291464 | tf_op jit(solution)/shard_map/ppermute | solution.py:39
  217.8 158.4 %collective-permute-start.6 = (bf16[2,4,256,512]{3,2,1,0:T(8,128)(2,1)}, bf16[2,4,256,512]{3,2,1,0:T(8,128)(2,1)}, u32[]{:S(2)}, u32[]{:S(2)}) collective-permute-start(bf16[2,4,256,512]{3,2,1,0:T(8,128)(2,1)} %pad_maximum_fusion), channel_id=1, source_target_pairs={{0,64},{4,68},{8,72},{12,76},{16,80},{20,84},{24,88},{28,92},{32,9... | collective-permute-start | bytes 6291464 | tf_op jit(solution)/shard_map/ppermute | solution.py:39
  368.7 2.5 copy-start.1
Sparse Core Ops, SparseCore 0:
  9.1 359.5 all-gather.3
  370.5 388.3 all-gather.5
  760.7 297.1 all-gather.7
